TPU v7x, 32 devices: a whole 2x2x4 slice. The times are simulated.
32 devices in a mesh: chan: 16 (over z, x, core), win: 2 (over y).
Axes of the slice: x: 2, y: 2, z: 4, core: 2. Of those that a mesh axis runs over, the one named last changes fastest.
Arguments:
- traces: float32 [512, 4, 1024], P('chan', 'win'), may hold values from -100 to 100, as said below
- live_counts: int32 [16], P('chan'), may hold values from 1 to 32, as said below
- pair_lists: int32 [16, 4, 3], P('chan'), may hold values from 0 to 15, as said below
Outputs:
- correlations: float32 [1024, 64, 256], P('win', 'chan')
Inputs may be any that keep to these rules, and one draw needn't show every extreme that they name: `traces`: sum of a random-amplitude noise, a band tone and an offset for each channel and sub-window. `live_counts`: at least one block has all 32 channels live. `pair_lists`: the valid slots of an owner come first, 1 to 4 of them, and some owner has all 4; in a valid slot the first block is at most the second; padded slots are (0, 0, 0).
All inputs are finite; a program needn't handle non-finite values.
Results may differ from a plain program's by a relative error of at most 0.000073.
Values sent between devices are 32-bit elements; how exact they have to be, the bound alone decides.
A program may use at most 128 MiB of HBM per device.

v0:
```python
import functools
import math

import jax
import jax.numpy as jnp
import ml_dtypes
import numpy as np
from jax import lax
from jax.experimental import pallas as pl
from jax.experimental.pallas import tpu as pltpu
from jax.sharding import PartitionSpec as P

SAMP = 1024
F0 = 2
NF = 128
NLAG = 256
LANES = 128
MESH = pl.DeviceIdType.MESH


def split_table(table):
    high = table.astype(np.float32).astype(ml_dtypes.bfloat16)
    low = (table - high.astype(np.float64)).astype(np.float32).astype(ml_dtypes.bfloat16)
    return high, low


@functools.lru_cache
def forward_tables():
    samples = np.arange(SAMP)
    bins = F0 + np.arange(NF)
    angles = (samples[:, None] * bins[None, :] % SAMP) * (2.0 * math.pi / SAMP)
    taper = 0.5 - 0.5 * np.cos(samples * (2.0 * math.pi / SAMP))
    return split_table(taper[:, None] * np.concatenate([np.cos(angles), -np.sin(angles)], axis=1))


@functools.lru_cache
def inverse_tables(window_total):
    bins = F0 + np.arange(NF)
    lags = np.arange(NLAG) - NLAG // 2
    angles = (bins[:, None] * lags[None, :] % SAMP) * (2.0 * math.pi / SAMP)
    table = np.concatenate([np.cos(angles), -np.sin(angles)], axis=0)
    return split_table(table / math.sqrt(window_total * NF))


def split(value):
    high = value.astype(jnp.bfloat16)
    return high, (value - high.astype(jnp.float32)).astype(jnp.bfloat16)


def dot(left, right):
    return jnp.dot(left, right, preferred_element_type=jnp.float32)


def whitened(block, windows, count_ref, traces_ref, high_ref, low_ref):
    tiles = SAMP // LANES
    parts = []
    for w in range(windows):
        pieces = [
            traces_ref[pl.ds(tile * windows + w, block, stride=tiles * windows), :]
            for tile in range(tiles)
        ]
        parts.append(jnp.concatenate(pieces, axis=1))
    samples = jnp.concatenate(parts, axis=0)
    centred = samples - jnp.sum(samples, axis=1, keepdims=True) * (1.0 / SAMP)
    high, low = split(centred)
    spectra = dot(high, high_ref[...]) + dot(low, high_ref[...]) + dot(high, low_ref[...])
    power = jnp.sum(spectra * spectra, axis=1, keepdims=True) * (1.0 / NF)
    channel = lax.broadcasted_iota(jnp.int32, (windows * block, 1), 0) % block
    live = (channel < count_ref[0]).astype(jnp.float32)
    return spectra * (live / jnp.sqrt(power + 1e-06))


def white_kernel(block, windows, count_ref, traces_ref, high_ref, low_ref, out_ref):
    out_ref[...] = whitened(block, windows, count_ref, traces_ref, high_ref, low_ref)


def gather_kernel(
    block, windows, z_total, count_ref, traces_ref, high_ref, low_ref, held,
    z_send, z_recv, x_send, x_recv, y_send, y_recv, f_send, f_recv, s_send, s_recv,
):
    me = lax.axis_index("chan")
    y = lax.axis_index("win")
    z, x, core = me // 4, (me // 2) % 2, me % 2

    def chan_of(z_at, x_at, core_at):
        return z_at * 4 + x_at * 2 + core_at

    along_z = [((z + d) % z_total) for d in range(z_total)]
    x_peer = (chan_of(z, 1 - x, core), y)
    y_peer = (me, 1 - y)
    sibling = (chan_of(z, x, 1 - core), y)
    barrier = pltpu.get_barrier_semaphore()
    peers = [(chan_of(along_z[d], x, core), y) for d in range(1, z_total)]
    peers += [x_peer, y_peer, sibling]
    for peer in peers:
        pl.semaphore_signal(barrier, inc=1, device_id=peer, device_id_type=MESH)

    held[y, me] = whitened(block, windows, count_ref, traces_ref, high_ref, low_ref)
    pl.semaphore_wait(barrier, len(peers))

    sent = []
    incoming = {}

    def send(y_at, chan_at, send_sem, recv_sem, peer):
        copy = pltpu.make_async_remote_copy(
            src_ref=held.at[y_at, chan_at],
            dst_ref=held.at[y_at, chan_at],
            send_sem=send_sem,
            recv_sem=recv_sem,
            device_id=peer,
            device_id_type=MESH,
        )
        copy.start()
        sent.append(copy)
        return copy

    def to_sibling(slot, y_at, chan_at):
        send(y_at, chan_at, s_send.at[slot], s_recv.at[slot], sibling)

    send(y, me, x_send.at[0], x_recv.at[0], x_peer)
    send(y, me, y_send.at[0], y_recv.at[0], y_peer)
    z_copies = [None]
    for d in range(1, z_total):
        to_z = (z + z_total - d) % z_total
        z_copies.append(send(y, me, z_send.at[d], z_recv.at[d], (chan_of(to_z, x, core), y)))
    to_sibling(0, y, me)

    def wait_arrival(recv_sem):
        pltpu.make_async_copy(held.at[y, me], held.at[y, me], recv_sem).wait()

    for d in range(z_total):
        column = chan_of(along_z[d], x, core)
        across = chan_of(along_z[d], 1 - x, core)
        if d > 0:
            z_copies[d].wait_recv()
            send(y, column, x_send.at[d], x_recv.at[d], x_peer)
            send(y, column, y_send.at[d], y_recv.at[d], y_peer)
            to_sibling(4 * d, y, column)
        wait_arrival(x_recv.at[d])
        if d % 2 == 0:
            send(y, across, f_send.at[d], f_recv.at[d], y_peer)
        to_sibling(4 * d + 1, y, across)
        wait_arrival(y_recv.at[d])
        if d % 2 == 1:
            send(1 - y, column, f_send.at[d], f_recv.at[d], x_peer)
        to_sibling(4 * d + 2, 1 - y, column)
    for d in range(z_total):
        wait_arrival(f_recv.at[d])
        to_sibling(4 * d + 3, 1 - y, chan_of(along_z[d], 1 - x, core))
    for slot in range(4 * z_total):
        wait_arrival(s_recv.at[slot])
    for copy in sent:
        copy.wait_send()


def lag_kernel(block, chunk, slots, pairs_ref, place_ref, *refs):
    firsts, seconds = refs[:slots], refs[slots : 2 * slots]
    high_table, low_table, out_ref, high_ref, low_ref = refs[2 * slots :]
    rows = chunk * block
    y_total, _, local = firsts[0].shape[:3]
    windows = [(yy, ww) for yy in range(y_total) for ww in range(local // block)]
    start = place_ref[0] + pl.program_id(0) * chunk
    for p in range(slots):
        valid = pairs_ref[3 * p + 2].astype(jnp.float32)
        for i in range(chunk):
            real = jnp.zeros((block, NF), jnp.float32)
            imag = jnp.zeros((block, NF), jnp.float32)
            for yy, ww in windows:
                a = firsts[p][yy, 0, pl.ds(ww * block + start + i, 1), :] * valid
                real_a, imag_a = a[:, :NF], a[:, NF:]
                real_b = seconds[p][yy, 0, ww * block : (ww + 1) * block, :NF]
                imag_b = seconds[p][yy, 0, ww * block : (ww + 1) * block, NF:]
                real = real + (real_a * real_b + imag_a * imag_b)
                imag = imag + (imag_a * real_b - real_a * imag_b)
            at = pl.ds(p * rows + i * block, block)
            high_ref[at, :NF], low_ref[at, :NF] = split(real)
            high_ref[at, NF:], low_ref[at, NF:] = split(imag)
    for p in range(slots):
        at = pl.ds(p * rows, rows)
        high, low = high_ref[at, :], low_ref[at, :]
        lagged = dot(high, high_table[...]) + dot(low, high_table[...]) + dot(high, low_table[...])
        for h in range(NLAG // LANES):
            out_ref[pl.ds(h * slots + p, rows, stride=slots * (NLAG // LANES)), :] = lagged[
                :, h * LANES : (h + 1) * LANES
            ]


def body(routed, chan_total, win_total, traces, live_counts, pair_lists):
    block, windows, samples = traces.shape
    slots = pair_lists.shape[1]
    high, low = (jnp.asarray(t) for t in forward_tables())
    tiles = samples // LANES
    linear = traces.reshape(block, windows, tiles, LANES).transpose(0, 2, 1, 3)
    linear = linear.reshape(block * tiles * windows, LANES)
    vmem = pl.BlockSpec(memory_space=pltpu.VMEM)
    smem = pl.BlockSpec(memory_space=pltpu.SMEM)
    local = windows * block
    if routed:
        z_total = chan_total // 4
        dma = pltpu.SemaphoreType.DMA
        held = pl.pallas_call(
            functools.partial(gather_kernel, block, windows, z_total),
            out_shape=jax.ShapeDtypeStruct((win_total, chan_total, local, 2 * NF), jnp.float32),
            in_specs=[smem, vmem, vmem, vmem],
            out_specs=vmem,
            scratch_shapes=[dma((z_total,))] * 8 + [dma((4 * z_total,))] * 2,
            compiler_params=pltpu.CompilerParams(
                collective_id=0, has_side_effects=True, vmem_limit_bytes=24 * 2**20
            ),
            name="whiten_gather",
        )(live_counts, linear, high, low)
    else:
        white = pl.pallas_call(
            functools.partial(white_kernel, block, windows),
            out_shape=jax.ShapeDtypeStruct((local, 2 * NF), jnp.float32),
            in_specs=[smem, vmem, vmem, vmem],
            out_specs=vmem,
            compiler_params=pltpu.CompilerParams(vmem_limit_bytes=24 * 2**20),
            name="whiten",
        )(live_counts, linear, high, low)
        held = lax.all_gather(white, ("win", "chan"), axis=0, tiled=False)
        held = held.reshape(win_total, chan_total, local, 2 * NF)

    firsts = block // win_total
    chunk = min(4, firsts)
    rows = chunk * block
    inv_high, inv_low = (jnp.asarray(t) for t in inverse_tables(windows * win_total))
    place = (lax.axis_index("win") * firsts).astype(jnp.int32).reshape(1)
    pairs = pair_lists.reshape(slots * 3)
    spec = (win_total, 1, local, 2 * NF)

    def block_spec(entry):
        return pl.BlockSpec(spec, lambda g, pairs, place: (0, pairs[entry], 0, 0))

    table_spec = pl.BlockSpec((2 * NF, NLAG), lambda g, pairs, place: (0, 0))
    tall = slots * (NLAG // LANES)
    out = pl.pallas_call(
        functools.partial(lag_kernel, block, chunk, slots),
        out_shape=jax.ShapeDtypeStruct((firsts * block * tall, LANES), jnp.float32),
        grid_spec=pltpu.PrefetchScalarGridSpec(
            num_scalar_prefetch=2,
            grid=(firsts // chunk,),
            in_specs=[block_spec(3 * p) for p in range(slots)]
            + [block_spec(3 * p + 1) for p in range(slots)]
            + [table_spec, table_spec],
            out_specs=pl.BlockSpec((rows * tall, LANES), lambda g, pairs, place: (g, 0)),
            scratch_shapes=[pltpu.VMEM((slots * rows, 2 * NF), jnp.bfloat16)] * 2,
        ),
        compiler_params=pltpu.CompilerParams(vmem_limit_bytes=32 * 2**20),
        name="cross_lags",
    )(pairs, place, *([held] * (2 * slots)), inv_high, inv_low)
    out = out.reshape(firsts * block, NLAG // LANES, slots, LANES).transpose(0, 2, 1, 3)
    return out.reshape(firsts * block, slots, NLAG)


def solution(mesh):
    chan_total, win_total = mesh.shape["chan"], mesh.shape["win"]
    routed = (chan_total, win_total) == (16, 2)
    return jax.shard_map(
        functools.partial(body, routed, chan_total, win_total),
        mesh=mesh,
        in_specs=(P("chan", "win", None), P("chan"), P("chan", None, None)),
        out_specs=P("win", "chan", None),
        check_vma=False,
    )
```

profile of v0, /device:TPU:0, one launch (start us, length us, event | category | flops | bytes accessed | tf_op | source)
XLA Modules:
  0.0 35.1 jit_solution(4806955438398882731)
XLA Ops:
  0.7 0.8 %copy.11 = s32[1,4,3]{2,1,0:T(4,128)S(1)} copy(s32[1,4,3]{1,0,2:T(1,128)} %param.9) | data formatting | bytes 96 | tf_op args[2]
  1.4 0.1 reshape.18.pairs_ref
  1.5 0.0 copy-start
  1.5 1.0 %copy-done = bf16[1024,256]{1,0:T(8,128)(2,1)S(1)} copy-done((bf16[1024,256]{1,0:T(8,128)(2,1)S(1)}, bf16[1024,256]{1,0:T(8,128)(2,1)}, u32[]{:S(2)}) %copy-start) | copy-done | bytes 524312
  2.5 0.0 copy-start.1
  2.6 1.0 %copy-done.1 = bf16[1024,256]{1,0:T(8,128)(2,1)S(1)} copy-done((bf16[1024,256]{1,0:T(8,128)(2,1)S(1)}, bf16[1024,256]{1,0:T(8,128)(2,1)}, u32[]{:S(2)}) %copy-start.1) | copy-done | bytes 524312
  3.6 0.0 copy-start.2
  3.6 0.9 %copy-done.2 = f32[32,2,1024]{2,1,0:T(2,128)S(1)} copy-done((f32[32,2,1024]{2,1,0:T(2,128)S(1)}, f32[32,2,1024]{2,1,0:T(2,128)}, u32[]{:S(2)}) %copy-start.2) | copy-done | bytes 262168
  4.5 0.0 copy-start.3
  4.5 0.0 copy-start.4
  4.5 26.1 %whiten_gather.1.refs_0_.refs_1_.refs_2_.refs_3_.refs_4_.refs_5_.refs_6_.refs_7_ = f32[2,16,64,256]{3,2,1,0:T(8,128)S(1)} custom-call(s32[1]{0:T(128)S(6)} %copy.14.count_ref, f32[512,128]{1,0:T(8,128)S(1)} %bitcast.11, bf16[1024,256]{1,0:T(8,128)(2,1)S(1)} %copy-done.1, bf16[1024,256]{1,0:T(8,128)(2,1)S(1)} %copy-done), custom_call_target="tpu_custom_call" | custom-call | tf_op jit(solution)/shard_map/whiten_gather/pallas_call | solution.py:201
  30.6 0.0 copy-done.3
  30.6 0.0 copy-done.4
  30.6 4.5 %cross_lags.1 = f32[4096,128]{1,0:T(8,128)} custom-call(s32[12]{0:T(128)S(1)} %reshape.18.pairs_ref, s32[1]{0:T(128)} %bitcast.place_ref, f32[2,16,64,256]{3,2,1,0:T(8,128)S(1)} %whiten_gather.1.refs_0_.refs_1_.refs_2_.refs_3_.refs_4_.refs_5_.refs_6_.refs_7_, ...), custom_call_target="tpu_custom_call" | custom-call | tf_op jit(solution)/shard_map/cross_lags/pallas_call | solution.py:237
Async XLA Ops:
  1.5 1.0 %copy-start = (bf16[1024,256]{1,0:T(8,128)(2,1)S(1)}, bf16[1024,256]{1,0:T(8,128)(2,1)}, u32[]{:S(2)}) copy-start(bf16[1024,256]{1,0:T(8,128)(2,1)} %constant.15.clone.low_ref) | copy-start | bytes 1572868
  2.5 1.0 %copy-start.1 = (bf16[1024,256]{1,0:T(8,128)(2,1)S(1)}, bf16[1024,256]{1,0:T(8,128)(2,1)}, u32[]{:S(2)}) copy-start(bf16[1024,256]{1,0:T(8,128)(2,1)} %constant.14.clone.high_ref) | copy-start | bytes 1572868
  3.6 0.9 %copy-start.2 = (f32[32,2,1024]{2,1,0:T(2,128)S(1)}, f32[32,2,1024]{2,1,0:T(2,128)}, u32[]{:S(2)}) copy-start(f32[32,2,1024]{2,1,0:T(2,128)} %param.7) | copy-start | bytes 786436
  4.5 26.1 %copy-start.3 = (bf16[256,256]{1,0:T(8,128)(2,1)S(1)}, bf16[256,256]{1,0:T(8,128)(2,1)}, u32[]{:S(2)}) copy-start(bf16[256,256]{1,0:T(8,128)(2,1)} %constant.17.clone.refs_9_) | copy-start | bytes 393220
  4.5 26.1 %copy-start.4 = (bf16[256,256]{1,0:T(8,128)(2,1)S(1)}, bf16[256,256]{1,0:T(8,128)(2,1)}, u32[]{:S(2)}) copy-start(bf16[256,256]{1,0:T(8,128)(2,1)} %constant.16.clone.refs_8_) | copy-start | bytes 393220
where the time goes:
time: 35.4 us; the launch traced here: 35.1 us
  Pallas kernels  30.5 us (86%)
  local copies, waits for them, and re-layouts  3.89 us (11%)
  between operations  0.68 us (2%)
    pallas_call x1, Pallas kernels, body(): pl.pallas_call(functools.partial(gather_kernel, block, windows, z_total),...  26.1 us
    pallas_call x1, Pallas kernels, body(): pl.pallas_call(functools.partial(lag_kernel, block, chunk, slots), out_sh...  4.46 us
    unnamed x11, local copies, waits for them, and re-layouts  3.81 us

commit v1 on v0

--- a/solution.py
+++ b/solution.py
@@ -75,9 +75,17 @@
 
 
 def gather_kernel(
-    block, windows, z_total, count_ref, traces_ref, high_ref, low_ref, held,
-    z_send, z_recv, x_send, x_recv, y_send, y_recv, f_send, f_recv, s_send, s_recv,
+    block, windows, count_ref, traces_hbm, high_hbm, low_hbm, held, traces_ref, high_ref, low_ref,
+    load, send_sem, link_recv, core_recv,
 ):
+    loads = [
+        pltpu.make_async_copy(source, target, load.at[i])
+        for i, (source, target) in enumerate(
+            [(traces_hbm, traces_ref), (high_hbm, high_ref), (low_hbm, low_ref)]
+        )
+    ]
+    for copy in loads:
+        copy.start()
     me = lax.axis_index("chan")
     y = lax.axis_index("win")
     z, x, core = me // 4, (me // 2) % 2, me % 2
@@ -85,70 +93,90 @@
     def chan_of(z_at, x_at, core_at):
         return z_at * 4 + x_at * 2 + core_at
 
-    along_z = [((z + d) % z_total) for d in range(z_total)]
+    upper = z // 2
+    pair = z + 1 - 2 * (z % 2)
+    near, far = 2 - upper, 3 - 3 * upper
     x_peer = (chan_of(z, 1 - x, core), y)
     y_peer = (me, 1 - y)
+    diagonal = (chan_of(z, 1 - x, core), 1 - y)
     sibling = (chan_of(z, x, 1 - core), y)
+    pair_peer, near_peer, far_peer = ((chan_of(at, x, core), y) for at in (pair, near, far))
     barrier = pltpu.get_barrier_semaphore()
-    peers = [(chan_of(along_z[d], x, core), y) for d in range(1, z_total)]
-    peers += [x_peer, y_peer, sibling]
+    peers = (x_peer, y_peer, diagonal, sibling, pair_peer, near_peer, far_peer)
     for peer in peers:
         pl.semaphore_signal(barrier, inc=1, device_id=peer, device_id_type=MESH)
-
+    for copy in loads:
+        copy.wait()
     held[y, me] = whitened(block, windows, count_ref, traces_ref, high_ref, low_ref)
     pl.semaphore_wait(barrier, len(peers))
 
     sent = []
-    incoming = {}
-
-    def send(y_at, chan_at, send_sem, recv_sem, peer):
+
+    def shard(z_at, kind, core_at):
+        x_at = x if kind % 2 == 0 else 1 - x
+        y_at = y if kind < 2 else 1 - y
+        return held.at[y_at, chan_of(z_at, x_at, core_at)]
+
+    def send(part, recv_sem, peer):
         copy = pltpu.make_async_remote_copy(
-            src_ref=held.at[y_at, chan_at],
-            dst_ref=held.at[y_at, chan_at],
-            send_sem=send_sem,
+            src_ref=part,
+            dst_ref=part,
+            send_sem=send_sem.at[len(sent)],
             recv_sem=recv_sem,
             device_id=peer,
             device_id_type=MESH,
         )
         copy.start()
         sent.append(copy)
-        return copy
-
-    def to_sibling(slot, y_at, chan_at):
-        send(y_at, chan_at, s_send.at[slot], s_recv.at[slot], sibling)
-
-    send(y, me, x_send.at[0], x_recv.at[0], x_peer)
-    send(y, me, y_send.at[0], y_recv.at[0], y_peer)
-    z_copies = [None]
-    for d in range(1, z_total):
-        to_z = (z + z_total - d) % z_total
-        z_copies.append(send(y, me, z_send.at[d], z_recv.at[d], (chan_of(to_z, x, core), y)))
-    to_sibling(0, y, me)
-
-    def wait_arrival(recv_sem):
-        pltpu.make_async_copy(held.at[y, me], held.at[y, me], recv_sem).wait()
-
-    for d in range(z_total):
-        column = chan_of(along_z[d], x, core)
-        across = chan_of(along_z[d], 1 - x, core)
-        if d > 0:
-            z_copies[d].wait_recv()
-            send(y, column, x_send.at[d], x_recv.at[d], x_peer)
-            send(y, column, y_send.at[d], y_recv.at[d], y_peer)
-            to_sibling(4 * d, y, column)
-        wait_arrival(x_recv.at[d])
-        if d % 2 == 0:
-            send(y, across, f_send.at[d], f_recv.at[d], y_peer)
-        to_sibling(4 * d + 1, y, across)
-        wait_arrival(y_recv.at[d])
-        if d % 2 == 1:
-            send(1 - y, column, f_send.at[d], f_recv.at[d], x_peer)
-        to_sibling(4 * d + 2, 1 - y, column)
-    for d in range(z_total):
-        wait_arrival(f_recv.at[d])
-        to_sibling(4 * d + 3, 1 - y, chan_of(along_z[d], 1 - x, core))
-    for slot in range(4 * z_total):
-        wait_arrival(s_recv.at[slot])
+
+    def to_link(z_at, kind, kind_there, peer):
+        send(shard(z_at, kind, core), link_recv.at[4 * z_at + kind_there], peer)
+
+    def to_core(z_at, kind):
+        send(shard(z_at, kind, core), core_recv.at[4 * z_at + kind], sibling)
+
+    def arrived(z_at, kind):
+        part = shard(z_at, kind, core)
+        pltpu.make_async_copy(part, part, link_recv.at[4 * z_at + kind]).wait()
+
+    to_link(z, 0, 0, near_peer)
+    to_link(z, 0, 1, x_peer)
+    to_link(z, 0, 2, y_peer)
+    to_link(z, 0, 0, far_peer)
+    to_link(z, 0, 3, diagonal)
+    to_link(z, 0, 0, pair_peer)
+    to_core(z, 0)
+
+    def hand_to_pair(kind):
+        arrived(z, kind)
+        to_link(z, kind, kind, pair_peer)
+        to_core(z, kind)
+
+    def spread(z_at):
+        arrived(z_at, 0)
+        to_link(z_at, 0, 1, x_peer)
+        to_link(z_at, 0, 2, y_peer)
+        to_link(z_at, 0, 3, diagonal)
+        to_core(z_at, 0)
+
+    def hand_on(z_at, kind):
+        arrived(z_at, kind)
+        to_core(z_at, kind)
+
+    hand_to_pair(1)
+    hand_to_pair(2)
+    spread(near)
+    hand_to_pair(3)
+    spread(far)
+    for kind in range(4):
+        hand_on(pair, kind)
+    for z_at in (near, far):
+        for kind in range(1, 4):
+            hand_on(z_at, kind)
+    for z_at in range(4):
+        for kind in range(4):
+            part = shard(z_at, kind, 1 - core)
+            pltpu.make_async_copy(part, part, core_recv.at[4 * z_at + kind]).wait()
     for copy in sent:
         copy.wait_send()
 
@@ -161,7 +189,7 @@
     windows = [(yy, ww) for yy in range(y_total) for ww in range(local // block)]
     start = place_ref[0] + pl.program_id(0) * chunk
     for p in range(slots):
-        valid = pairs_ref[3 * p + 2].astype(jnp.float32)
+        valid = pairs_ref[2, 0, p].astype(jnp.float32)
         for i in range(chunk):
             real = jnp.zeros((block, NF), jnp.float32)
             imag = jnp.zeros((block, NF), jnp.float32)
@@ -196,19 +224,31 @@
     smem = pl.BlockSpec(memory_space=pltpu.SMEM)
     local = windows * block
     if routed:
-        z_total = chan_total // 4
         dma = pltpu.SemaphoreType.DMA
+        hbm = pl.BlockSpec(memory_space=pltpu.MemorySpace.HBM)
+
+        def in_hbm(value):
+            return pltpu.with_memory_space_constraint(value, pltpu.MemorySpace.HBM)
+
         held = pl.pallas_call(
-            functools.partial(gather_kernel, block, windows, z_total),
+            functools.partial(gather_kernel, block, windows),
             out_shape=jax.ShapeDtypeStruct((win_total, chan_total, local, 2 * NF), jnp.float32),
-            in_specs=[smem, vmem, vmem, vmem],
+            in_specs=[smem, hbm, hbm, hbm],
             out_specs=vmem,
-            scratch_shapes=[dma((z_total,))] * 8 + [dma((4 * z_total,))] * 2,
+            scratch_shapes=[
+                pltpu.VMEM(linear.shape, linear.dtype),
+                pltpu.VMEM(high.shape, high.dtype),
+                pltpu.VMEM(low.shape, low.dtype),
+                dma((3,)),
+                dma((31,)),
+                dma((16,)),
+                dma((16,)),
+            ],
             compiler_params=pltpu.CompilerParams(
                 collective_id=0, has_side_effects=True, vmem_limit_bytes=24 * 2**20
             ),
             name="whiten_gather",
-        )(live_counts, linear, high, low)
+        )(live_counts, *(in_hbm(value) for value in (linear, high, low)))
     else:
         white = pl.pallas_call(
             functools.partial(white_kernel, block, windows),
@@ -226,11 +266,11 @@
     rows = chunk * block
     inv_high, inv_low = (jnp.asarray(t) for t in inverse_tables(windows * win_total))
     place = (lax.axis_index("win") * firsts).astype(jnp.int32).reshape(1)
-    pairs = pair_lists.reshape(slots * 3)
+    pairs = pair_lists.transpose(2, 0, 1)
     spec = (win_total, 1, local, 2 * NF)
 
-    def block_spec(entry):
-        return pl.BlockSpec(spec, lambda g, pairs, place: (0, pairs[entry], 0, 0))
+    def block_spec(entry, p):
+        return pl.BlockSpec(spec, lambda g, pairs, place: (0, pairs[entry, 0, p], 0, 0))
 
     table_spec = pl.BlockSpec((2 * NF, NLAG), lambda g, pairs, place: (0, 0))
     tall = slots * (NLAG // LANES)
@@ -240,8 +280,8 @@
         grid_spec=pltpu.PrefetchScalarGridSpec(
             num_scalar_prefetch=2,
             grid=(firsts // chunk,),
-            in_specs=[block_spec(3 * p) for p in range(slots)]
-            + [block_spec(3 * p + 1) for p in range(slots)]
+            in_specs=[block_spec(0, p) for p in range(slots)]
+            + [block_spec(1, p) for p in range(slots)]
             + [table_spec, table_spec],
             out_specs=pl.BlockSpec((rows * tall, LANES), lambda g, pairs, place: (g, 0)),
             scratch_shapes=[pltpu.VMEM((slots * rows, 2 * NF), jnp.bfloat16)] * 2,

time: 35.4 us -> 27.1 us (0.77)
  Pallas kernels: 30.5 us -> 26.2 us
  local copies, waits for them, and re-layouts: 3.89 us -> 0.01 us
    pallas_call x1, Pallas kernels: 26.1 us -> 21.8 us  [body(): pl.pallas_call(functools.partial(gather_kernel, block, windows), out_shap...]
    unnamed x11 -> x6, local copies, waits for them, and re-layouts: 3.81 us -> 0.01 us
where the time goes in v1:
time: 27.1 us; the launch traced here: 27 us
  Pallas kernels  26.2 us (97%)
  between operations  0.73 us (3%)
    pallas_call x1, Pallas kernels, body(): pl.pallas_call(functools.partial(gather_kernel, block, windows), out_shap...  21.8 us
    pallas_call x1, Pallas kernels, body(): pl.pallas_call(functools.partial(lag_kernel, block, chunk, slots), out_sh...  4.41 us

profile of v1, /device:TPU:0, one launch (start us, length us, event | category | flops | bytes accessed | tf_op | source)
XLA Modules:
  0.0 27.0 jit_solution(17247950016494672062)
XLA Ops:
  0.0 0.0 copy-start
  0.0 0.0 copy-start.1
  0.0 0.0 copy-start.2
  0.7 21.8 %whiten_gather.1.refs_0_.refs_1_.refs_2_.refs_3_.refs_4_.refs_5_.refs_6_.refs_7_ = f32[2,16,64,256]{3,2,1,0:T(8,128)S(1)} custom-call(s32[1]{0:T(128)S(6)} %copy.10.count_ref, f32[512,128]{1,0:T(8,128)} %bitcast.13, bf16[1024,256]{1,0:T(8,128)(2,1)} %constant.14.clone.high_hbm, bf16[1024,256]{1,0:T(8,128)(2,1)} %constant.15.clone.low_hbm), custom_call_target="tpu_custom_call" | custom-call | tf_op jit(solution)/shard_map/whiten_gather/pallas_call | solution.py:233
  22.5 0.0 copy-done
  22.5 0.0 copy-done.1
  22.5 0.0 copy-done.2
  22.6 4.4 %cross_lags.1 = f32[4096,128]{1,0:T(8,128)} custom-call(s32[3,1,4]{2,1,0:T(1,128)S(1)} %bitcast.12, s32[1]{0:T(128)} %bitcast.1.place_ref, f32[2,16,64,256]{3,2,1,0:T(8,128)S(1)} %whiten_gather.1.refs_0_.refs_1_.refs_2_.refs_3_.refs_4_.refs_5_.refs_6_.refs_7_, ...), custom_call_target="tpu_custom_call" | custom-call | tf_op jit(solution)/shard_map/cross_lags/pallas_call | solution.py:277
Async XLA Ops:
  0.0 22.5 %copy-start = (bf16[256,256]{1,0:T(8,128)(2,1)S(1)}, bf16[256,256]{1,0:T(8,128)(2,1)}, u32[]{:S(2)}) copy-start(bf16[256,256]{1,0:T(8,128)(2,1)} %constant.17.clone.refs_9_) | copy-start | bytes 393220
  0.0 22.5 %copy-start.1 = (bf16[256,256]{1,0:T(8,128)(2,1)S(1)}, bf16[256,256]{1,0:T(8,128)(2,1)}, u32[]{:S(2)}) copy-start(bf16[256,256]{1,0:T(8,128)(2,1)} %constant.16.clone.refs_8_) | copy-start | bytes 393220
  0.0 22.5 %copy-start.2 = (s32[1,4,3]{1,0,2:T(1,128)S(1)}, s32[1,4,3]{1,0,2:T(1,128)}, u32[]{:S(2)}) copy-start(s32[1,4,3]{1,0,2:T(1,128)} %param.9) | copy-start | bytes 148

commit v2 on v1

--- a/solution.py
+++ b/solution.py
@@ -181,36 +181,58 @@
         copy.wait_send()
 
 
-def lag_kernel(block, chunk, slots, pairs_ref, place_ref, *refs):
-    firsts, seconds = refs[:slots], refs[slots : 2 * slots]
-    high_table, low_table, out_ref, high_ref, low_ref = refs[2 * slots :]
+def lag_kernel(
+    block, chunk, slots, pairs_ref, place_ref, held_ref, high_table, low_table, out_hbm,
+    high_ref, low_ref, out_ref, stored,
+):
     rows = chunk * block
-    y_total, _, local = firsts[0].shape[:3]
+    tall = slots * (NLAG // LANES)
+    y_total, _, local = held_ref.shape[:3]
     windows = [(yy, ww) for yy in range(y_total) for ww in range(local // block)]
-    start = place_ref[0] + pl.program_id(0) * chunk
-    for p in range(slots):
-        valid = pairs_ref[2, 0, p].astype(jnp.float32)
-        for i in range(chunk):
-            real = jnp.zeros((block, NF), jnp.float32)
-            imag = jnp.zeros((block, NF), jnp.float32)
-            for yy, ww in windows:
-                a = firsts[p][yy, 0, pl.ds(ww * block + start + i, 1), :] * valid
-                real_a, imag_a = a[:, :NF], a[:, NF:]
-                real_b = seconds[p][yy, 0, ww * block : (ww + 1) * block, :NF]
-                imag_b = seconds[p][yy, 0, ww * block : (ww + 1) * block, NF:]
-                real = real + (real_a * real_b + imag_a * imag_b)
-                imag = imag + (imag_a * real_b - real_a * imag_b)
-            at = pl.ds(p * rows + i * block, block)
-            high_ref[at, :NF], low_ref[at, :NF] = split(real)
-            high_ref[at, NF:], low_ref[at, NF:] = split(imag)
-    for p in range(slots):
-        at = pl.ds(p * rows, rows)
-        high, low = high_ref[at, :], low_ref[at, :]
-        lagged = dot(high, high_table[...]) + dot(low, high_table[...]) + dot(high, low_table[...])
-        for h in range(NLAG // LANES):
-            out_ref[pl.ds(h * slots + p, rows, stride=slots * (NLAG // LANES)), :] = lagged[
-                :, h * LANES : (h + 1) * LANES
-            ]
+    groups = out_ref.shape[0]
+
+    def store(group):
+        return pltpu.make_async_copy(
+            out_ref.at[group],
+            out_hbm.at[pl.ds(group * (rows * tall), rows * tall)],
+            stored.at[group],
+        )
+
+    def make_group(group, carry):
+        start = place_ref[0] + group * chunk
+        for p in range(slots):
+            first, second = pairs_ref[0, 0, p], pairs_ref[1, 0, p]
+            valid = pairs_ref[2, 0, p].astype(jnp.float32)
+            for i in range(0, chunk, 2):
+                real = [jnp.zeros((block, NF), jnp.float32)] * 2
+                imag = [jnp.zeros((block, NF), jnp.float32)] * 2
+                for yy, ww in windows:
+                    real_b = held_ref[yy, second, ww * block : (ww + 1) * block, :NF]
+                    imag_b = held_ref[yy, second, ww * block : (ww + 1) * block, NF:]
+                    for j in range(2):
+                        a = held_ref[yy, first, pl.ds(ww * block + start + i + j, 1), :] * valid
+                        real_a, imag_a = a[:, :NF], a[:, NF:]
+                        real[j] = real[j] + (real_a * real_b + imag_a * imag_b)
+                        imag[j] = imag[j] + (imag_a * real_b - real_a * imag_b)
+                for j in range(2):
+                    at = pl.ds(p * rows + (i + j) * block, block)
+                    high_ref[at, :NF], low_ref[at, :NF] = split(real[j])
+                    high_ref[at, NF:], low_ref[at, NF:] = split(imag[j])
+            at = pl.ds(p * rows, rows)
+            high, low = high_ref[at, :], low_ref[at, :]
+            lagged = (
+                dot(high, high_table[...]) + dot(low, high_table[...]) + dot(high, low_table[...])
+            )
+            for h in range(NLAG // LANES):
+                out_ref[group, pl.ds(h * slots + p, rows, stride=tall), :] = lagged[
+                    :, h * LANES : (h + 1) * LANES
+                ]
+        store(group).start()
+        return carry
+
+    lax.fori_loop(0, groups, make_group, 0)
+    for group in range(groups):
+        store(group).wait()
 
 
 def body(routed, chan_total, win_total, traces, live_counts, pair_lists):
@@ -260,6 +282,7 @@
         )(live_counts, linear, high, low)
         held = lax.all_gather(white, ("win", "chan"), axis=0, tiled=False)
         held = held.reshape(win_total, chan_total, local, 2 * NF)
+        held = jnp.take(held, pair_lists[0, :, :2].T.reshape(2 * slots), axis=1, mode="clip")
 
     firsts = block // win_total
     chunk = min(4, firsts)
@@ -267,28 +290,25 @@
     inv_high, inv_low = (jnp.asarray(t) for t in inverse_tables(windows * win_total))
     place = (lax.axis_index("win") * firsts).astype(jnp.int32).reshape(1)
     pairs = pair_lists.transpose(2, 0, 1)
-    spec = (win_total, 1, local, 2 * NF)
-
-    def block_spec(entry, p):
-        return pl.BlockSpec(spec, lambda g, pairs, place: (0, pairs[entry, 0, p], 0, 0))
-
-    table_spec = pl.BlockSpec((2 * NF, NLAG), lambda g, pairs, place: (0, 0))
+    if not routed:
+        places = jnp.arange(2 * slots, dtype=pairs.dtype).reshape(2, 1, slots)
+        pairs = jnp.concatenate([places, pairs[2:]], axis=0)
     tall = slots * (NLAG // LANES)
+    groups = firsts // chunk
     out = pl.pallas_call(
         functools.partial(lag_kernel, block, chunk, slots),
         out_shape=jax.ShapeDtypeStruct((firsts * block * tall, LANES), jnp.float32),
-        grid_spec=pltpu.PrefetchScalarGridSpec(
-            num_scalar_prefetch=2,
-            grid=(firsts // chunk,),
-            in_specs=[block_spec(0, p) for p in range(slots)]
-            + [block_spec(1, p) for p in range(slots)]
-            + [table_spec, table_spec],
-            out_specs=pl.BlockSpec((rows * tall, LANES), lambda g, pairs, place: (g, 0)),
-            scratch_shapes=[pltpu.VMEM((slots * rows, 2 * NF), jnp.bfloat16)] * 2,
-        ),
+        in_specs=[smem, smem, vmem, vmem, vmem],
+        out_specs=pl.BlockSpec(memory_space=pltpu.MemorySpace.HBM),
+        scratch_shapes=[
+            pltpu.VMEM((slots * rows, 2 * NF), jnp.bfloat16),
+            pltpu.VMEM((slots * rows, 2 * NF), jnp.bfloat16),
+            pltpu.VMEM((groups, rows * tall, LANES), jnp.float32),
+            pltpu.SemaphoreType.DMA((groups,)),
+        ],
         compiler_params=pltpu.CompilerParams(vmem_limit_bytes=32 * 2**20),
         name="cross_lags",
-    )(pairs, place, *([held] * (2 * slots)), inv_high, inv_low)
+    )(pairs, place, held, inv_high, inv_low)
     out = out.reshape(firsts * block, NLAG // LANES, slots, LANES).transpose(0, 2, 1, 3)
     return out.reshape(firsts * block, slots, NLAG)
 

time: 27.1 us -> 26.8 us (0.989)
  Pallas kernels: 26.2 us -> 25.9 us
    pallas_call x1, Pallas kernels: 4.41 us -> 4.08 us  [body(): pl.pallas_call(functools.partial(lag_kernel, block, chunk, slots), out_sh...]
where the time goes in v2:
time: 26.8 us; the launch traced here: 26.6 us
  Pallas kernels  25.9 us (97%)
  between operations  0.73 us (3%)
    pallas_call x1, Pallas kernels, body(): pl.pallas_call(functools.partial(gather_kernel, block, windows), out_shap...  21.8 us
    pallas_call x1, Pallas kernels, body(): pl.pallas_call(functools.partial(lag_kernel, block, chunk, slots), out_sh...  4.08 us

profile of v2, /device:TPU:0, one launch (start us, length us, event | category | flops | bytes accessed | tf_op | source)
XLA Modules:
  0.0 26.6 jit_solution(12487300910956631479)
XLA Ops:
  0.0 0.0 copy-start
  0.0 0.0 copy-start.1
  0.0 0.0 copy-start.2
  0.7 21.8 %whiten_gather.1.held_ref = f32[2,16,64,256]{3,2,1,0:T(8,128)S(1)} custom-call(s32[1]{0:T(128)S(6)} %copy.10.count_ref, f32[512,128]{1,0:T(8,128)} %bitcast.13, bf16[1024,256]{1,0:T(8,128)(2,1)} %constant.14.clone.high_hbm, bf16[1024,256]{1,0:T(8,128)(2,1)} %constant.15.clone.low_hbm), custom_call_target="tpu_custom_call" | custom-call | tf_op jit(solution)/shard_map/whiten_gather/pallas_call | solution.py:255
  22.5 0.0 copy-done
  22.5 0.0 copy-done.1
  22.5 0.0 copy-done.2
  22.6 4.1 %cross_lags.1 = f32[4096,128]{1,0:T(8,128)} custom-call(s32[3,1,4]{2,1,0:T(1,128)S(1)} %bitcast.12, s32[1]{0:T(128)} %bitcast.1.place_ref, f32[2,16,64,256]{3,2,1,0:T(8,128)S(1)} %whiten_gather.1.held_ref, bf16[256,256]{1,0:T(8,128)(2,1)S(1)} %copy-done.1, bf16[256,256]{1,0:T(8,128)(2,1)S(1)} %copy-done), custom_call_target="tpu_custom_call" | custom-call | tf_op jit(solution)/shard_map/cross_lags/pallas_call | solution.py:298
Async XLA Ops:
  0.0 22.5 %copy-start = (bf16[256,256]{1,0:T(8,128)(2,1)S(1)}, bf16[256,256]{1,0:T(8,128)(2,1)}, u32[]{:S(2)}) copy-start(bf16[256,256]{1,0:T(8,128)(2,1)} %constant.17.clone.low_table) | copy-start | bytes 393220
  0.0 22.5 %copy-start.1 = (bf16[256,256]{1,0:T(8,128)(2,1)S(1)}, bf16[256,256]{1,0:T(8,128)(2,1)}, u32[]{:S(2)}) copy-start(bf16[256,256]{1,0:T(8,128)(2,1)} %constant.16.clone.high_table) | copy-start | bytes 393220
  0.0 22.5 %copy-start.2 = (s32[1,4,3]{1,0,2:T(1,128)S(1)}, s32[1,4,3]{1,0,2:T(1,128)}, u32[]{:S(2)}) copy-start(s32[1,4,3]{1,0,2:T(1,128)} %param.9) | copy-start | bytes 148
